TPU v7x, 32 devices: a whole 2x2x4 slice. The times are simulated.
32 devices in a mesh: parts: 2 (over y), clus: 4 (over z), sub: 4 (over x, core).
Axes of the slice: x: 2, y: 2, z: 4, core: 2. Of those that a mesh axis runs over, the one named last changes fastest.
Arguments:
- vector: bfloat16 [2, 16, 16384], P(None, None, ('parts', 'clus', 'sub')), parts along dimension 2, may hold values from -6 to 6
- near_blocks: bfloat16 [1536, 2, 128, 128], P(('parts', 'clus', 'sub')), parts along dimension 0, may hold values from -0.15625 to 0.15625
- near_rows: int32 [1536], P(('parts', 'clus', 'sub')), parts along dimension 0, may hold values from 0 to 63, as said below
- near_cols: int32 [1536], P(('parts', 'clus', 'sub')), parts along dimension 0, may hold values from 0 to 63, as said below
- row_basis: bfloat16 [2, 32, 16384], P(None, None, ('parts', 'clus', 'sub')), parts along dimension 2, may hold values from -0.75 to 0.75
- col_basis: bfloat16 [2, 32, 16384], P(None, None, ('parts', 'clus', 'sub')), parts along dimension 2, may hold values from -0.09375 to 0.09375
- couplings: bfloat16 [256, 2, 32, 32], P(('parts', 'clus', 'sub')), parts along dimension 0, may hold values from -0.125 to 0.125
- far_cols: int32 [256], P(('parts', 'clus', 'sub')), parts along dimension 0, may hold values from 0 to 3, as said below
Outputs:
- first_product: bfloat16 [2, 16, 16384], P(None, None, ('parts', 'clus', 'sub')), parts along dimension 2
- second_product: bfloat16 [2, 16, 16384], P(None, None, ('parts', 'clus', 'sub')), parts along dimension 2
There are 2 independent parts, one for each index of `parts`. A program takes and returns all parts, laid end to end along the dimension named above; each array names one. Nothing has to cross between parts.
Inputs may be any that keep to these rules, and one draw needn't show every extreme that they name: `near_rows`: the row leaf of a block lies in the subtree of the clus index that holds the block. `near_cols`: the column leaf of a block lies in its row leaf's subtree or an adjacent subtree, at most 16 leaves from the row leaf. `far_cols`: the column subtree of a pair of subtree s is never s.
All inputs are finite; a program needn't handle non-finite values.
Results may differ from a plain program's by a relative error of at most 0.017.
Values may be sent and summed in bfloat16 or wider, within the bound.
A program may use at most 64 MiB of HBM per device.

v0:
```python
import jax
import jax.numpy as jnp
from jax import lax
from jax.sharding import PartitionSpec as P


def padded(block, sides, width):
    for axis, dim in sides:
        count = lax.axis_size(axis)
        forward = [(i, i + 1) for i in range(count - 1)]
        backward = [(target, source) for source, target in forward]
        low = lax.ppermute(
            lax.slice_in_dim(block, block.shape[dim] - width, None, axis=dim), axis, forward
        )
        high = lax.ppermute(lax.slice_in_dim(block, 0, width, axis=dim), axis, backward)
        block = jnp.concatenate([low, block, high], axis=dim)
    return block


def combine(products):
    return jnp.stack([products[0, 0] - products[1, 1], products[0, 1] + products[1, 0]])


def per_device(
    vector, near_blocks, near_rows, near_cols, row_basis, col_basis, couplings, far_cols
):
    sub_count = lax.axis_size("sub")
    clus_id = lax.axis_index("clus")
    leaf_size = near_blocks.shape[-1]
    rhs_count = vector.shape[1]
    rows_dev = vector.shape[2]
    sub_rows = rows_dev * sub_count
    sub_leaves = sub_rows // leaf_size
    row_local = near_rows - clus_id * sub_leaves
    col_local = near_cols - (clus_id - 1) * sub_leaves
    row_onehot = (row_local[:, None] == jnp.arange(sub_leaves, dtype=jnp.int32)[None, :]).astype(
        jnp.float32
    )

    def apply_operator(current):
        subtree = lax.all_gather(current, "sub", axis=2, tiled=True)
        window = padded(subtree, (("clus", 2),), sub_rows)
        pieces = window.reshape(2, rhs_count, 3 * sub_leaves, leaf_size)
        picked = jnp.take(pieces, col_local, axis=2)
        products = jnp.einsum(
            "bqrc,pnbc->qpnbr", near_blocks, picked, preferred_element_type=jnp.float32
        )
        contrib = combine(products)
        spread = jnp.einsum("pnbr,bl->pnlr", contrib, row_onehot, precision=lax.Precision.HIGHEST)
        near_part = lax.psum_scatter(
            spread.reshape(2, rhs_count, sub_rows).astype(jnp.bfloat16),
            "sub",
            scatter_dimension=2,
            tiled=True,
        ).astype(jnp.float32)
        partial_value = combine(
            jnp.einsum("qkr,pnr->qpnk", col_basis, current, preferred_element_type=jnp.float32)
        )
        summed = lax.psum(partial_value, "sub")
        coefficients = lax.all_gather(summed.astype(jnp.bfloat16)[None], "clus", axis=0, tiled=True)
        picked_coeff = jnp.take(coefficients, far_cols, axis=0)
        coupled_terms = combine(
            jnp.einsum(
                "fqkj,fpnj->qpnk", couplings, picked_coeff, preferred_element_type=jnp.float32
            )
        )
        coupled = lax.psum(coupled_terms, "sub").astype(jnp.bfloat16)
        far_part = combine(
            jnp.einsum("qkr,pnk->qpnr", row_basis, coupled, preferred_element_type=jnp.float32)
        )
        return (near_part + far_part).astype(jnp.bfloat16)

    first_out = apply_operator(vector)
    second_out = apply_operator(first_out)
    return (first_out, second_out)


def solution(mesh):
    in_specs = (
        P(None, None, ("parts", "clus", "sub")),
        P(("parts", "clus", "sub"), None, None, None),
        P(("parts", "clus", "sub")),
        P(("parts", "clus", "sub")),
        P(None, None, ("parts", "clus", "sub")),
        P(None, None, ("parts", "clus", "sub")),
        P(("parts", "clus", "sub"), None, None, None),
        P(("parts", "clus", "sub")),
    )
    out_specs = (P(None, None, ("parts", "clus", "sub")), P(None, None, ("parts", "clus", "sub")))
    return jax.shard_map(
        per_device, mesh=mesh, in_specs=in_specs, out_specs=out_specs, check_vma=False
    )
```

profile of v0, /device:TPU:0, one launch (start us, length us, event | category | flops | bytes accessed | tf_op | source)
XLA Modules:
  0.0 173.7 jit_solution(9285898354810273459)
XLA Ops:
  7.2 6.8 %all_gather.12 = bf16[2,16,2048]{2,1,0:T(8,128)(2,1)S(1)} all-gather(bf16[2,16,512]{2,1,0:T(8,128)(2,1)} %param.12), channel_id=1, replica_groups=mesh['parts'=2,'clus'=4,'sub'=4] {'sub'}, dimensions={2}, use_global_device_ids=true | all-gather | bytes 163840 | tf_op jit(solution)/shard_map/all_gather | solution.py:41
  14.1 3.9 %collective-permute-start = (bf16[2,16,2048]{2,1,0:T(8,128)(2,1)S(1)}, bf16[2,16,2048]{2,1,0:T(8,128)(2,1)S(1)}, u32[]{:S(2)}, u32[]{:S(2)}) collective-permute-start(bf16[2,16,2048]{2,1,0:T(8,128)(2,1)S(1)} %all_gather.12), channel_id=1, source_target_pairs={{0,4},{4,8},{8,12},{1,5},{5,9},{9,13},{2,6},{6,10},{10,14},{3,7},{... | collective-permute-start | bytes 393224 | tf_op jit(solution)/shard_map/ppermute | solution.py:12
  17.9 1.3 collective-permute-start.1
  19.2 1.0 convolution_bitcast_fusion.5
  20.3 0.7 compare_select_fusion
  20.9 0.7 compare_and_fusion
  21.6 11.2 %psum.28 = bf16[2,16,32]{2,1,0:T(8,128)(2,1)S(1)} all-reduce(f32[2,16,32]{2,1,0:T(8,128)S(1)} %pad_maximum_fusion.2), channel_id=1, replica_groups=mesh['parts'=2,'clus'=4,'sub'=4] {'sub'}, use_global_device_ids=true, to_apply=%region_1.3 | all-reduce | flops 1024 | bytes 6144 | tf_op jit(solution)/shard_map/psum | solution.py:59
  32.8 14.6 %all-gather = bf16[8,16,32]{2,1,0:T(8,128)(2,1)S(1)} all-gather(bf16[2,16,32]{2,1,0:T(8,128)(2,1)S(1)} %psum.28), channel_id=2, replica_groups=mesh['parts'=2,'clus'=4,'sub'=4] {'clus'}, dimensions={0}, use_global_device_ids=true | all-gather | bytes 10240 | tf_op jit(solution)/shard_map/all_gather | solution.py:60
  48.0 1.1 convolution_bitcast_fusion.4
  49.2 10.3 %psum.29 = bf16[2,16,32]{2,1,0:T(8,128)(2,1)S(1)} all-reduce(f32[2,16,32]{2,1,0:T(8,128)S(1)} %pad_maximum_fusion.3), channel_id=1, replica_groups=mesh['parts'=2,'clus'=4,'sub'=4] {'sub'}, use_global_device_ids=true, to_apply=%region_2.0 | all-reduce | flops 1024 | bytes 6144 | tf_op jit(solution)/shard_map/psum | solution.py:67
  59.4 0.7 compare_and_fusion.1
  60.1 1.6 convolution_bitcast_fusion.1
  63.1 1.1 copy_bitcast_fusion.1
  64.2 1.4 gather_fusion
  65.5 2.2 %fusion.4 = f32[2,2,16,48,128]{4,2,0,1,3:T(8,128)S(1)} fusion(bf16[48,2,128,128]{3,2,1,0:T(8,128)(2,1)S(1)} %copy-done, bf16[48,2,16,128]{3,2,1,0:T(8,128)(2,1)} %gather_fusion, pred[48]{0:T(512)(128)(4,1)S(1)} %get-tuple-element.4), kind=kOutput, calls=%fused_computation.8 | convolution fusion | flops 100859904 | bytes 5111856 | tf_op jit(solution)/shard_map/bqrc,pnbc->qpnbr/dot_general | solution.py:45
  68.5 0.7 convert_element_type.45
  69.3 20.2 %reduce-scatter.3.cloned.1.call-done = bf16[2,16,512]{2,1,0:T(8,128)(2,1)} async-done(((bf16[2,16,2048]{2,1,0:T(8,128)(2,1)}), bf16[2,16,512]{2,1,0:T(8,128)(2,1)}) %reduce-scatter.3.cloned.1.call-update) | async-done | bytes 32784 | tf_op jit(solution)/shard_map/reduce_scatter | solution.py:50
  89.5 0.8 fusion.32
  90.3 5.4 %all_gather.14 = bf16[2,16,2048]{2,1,0:T(8,128)(2,1)S(1)} all-gather(bf16[2,16,512]{2,1,0:T(8,128)(2,1)S(1)} %fusion.32), channel_id=1, replica_groups=mesh['parts'=2,'clus'=4,'sub'=4] {'sub'}, dimensions={2}, use_global_device_ids=true | all-gather | bytes 163840 | tf_op jit(solution)/shard_map/all_gather | solution.py:41
  95.7 4.0 %collective-permute-start.2 = (bf16[2,16,2048]{2,1,0:T(8,128)(2,1)S(1)}, bf16[2,16,2048]{2,1,0:T(8,128)(2,1)}, u32[]{:S(2)}, u32[]{:S(2)}) collective-permute-start(bf16[2,16,2048]{2,1,0:T(8,128)(2,1)S(1)} %all_gather.14), channel_id=1, source_target_pairs={{0,4},{4,8},{8,12},{1,5},{5,9},{9,13},{2,6},{6,10},{10,14},{3,7},{... | collective-permute-start | bytes 393224 | tf_op jit(solution)/shard_map/ppermute | solution.py:12
  99.8 1.3 collective-permute-start.3
  101.3 10.6 %psum.30 = bf16[2,16,32]{2,1,0:T(8,128)(2,1)S(1)} all-reduce(f32[2,16,32]{2,1,0:T(8,128)S(1)} %pad_maximum_fusion.4), channel_id=1, replica_groups=mesh['parts'=2,'clus'=4,'sub'=4] {'sub'}, use_global_device_ids=true, to_apply=%region_4.7 | all-reduce | flops 1024 | bytes 6144 | tf_op jit(solution)/shard_map/psum | solution.py:59
  111.9 13.6 %all-gather.1 = bf16[8,16,32]{2,1,0:T(8,128)(2,1)S(1)} all-gather(bf16[2,16,32]{2,1,0:T(8,128)(2,1)S(1)} %psum.30), channel_id=3, replica_groups=mesh['parts'=2,'clus'=4,'sub'=4] {'clus'}, dimensions={0}, use_global_device_ids=true | all-gather | bytes 10240 | tf_op jit(solution)/shard_map/all_gather | solution.py:60
  126.0 1.2 convolution_bitcast_fusion.2
  127.3 10.1 %psum.31 = bf16[2,16,32]{2,1,0:T(8,128)(2,1)S(1)} all-reduce(f32[2,16,32]{2,1,0:T(8,128)S(1)} %pad_maximum_fusion.5), channel_id=1, replica_groups=mesh['parts'=2,'clus'=4,'sub'=4] {'sub'}, use_global_device_ids=true, to_apply=%region_5.8 | all-reduce | flops 1024 | bytes 6144 | tf_op jit(solution)/shard_map/psum | solution.py:67
  137.4 0.8 convolution_bitcast_fusion
  138.2 1.1 copy_bitcast_fusion
  139.3 1.4 gather_fusion.2
  140.7 2.2 %fusion.7 = f32[2,2,16,48,128]{4,2,0,1,3:T(8,128)S(1)} fusion(bf16[48,2,128,128]{3,2,1,0:T(8,128)(2,1)S(1)} %copy-done, bf16[48,2,16,128]{3,2,1,0:T(8,128)(2,1)} %gather_fusion.2, pred[48]{0:T(512)(128)(4,1)S(1)} %get-tuple-element.4), kind=kOutput, calls=%fused_computation.9 | convolution fusion | flops 100859904 | bytes 5111856 | tf_op jit(solution)/shard_map/bqrc,pnbc->qpnbr/dot_general | solution.py:45
  143.6 0.7 convert_element_type.52
  144.4 21.1 %reduce-scatter.5.cloned.1.call-done = bf16[2,16,512]{2,1,0:T(8,128)(2,1)} async-done(((bf16[2,16,2048]{2,1,0:T(8,128)(2,1)}), bf16[2,16,512]{2,1,0:T(8,128)(2,1)}) %reduce-scatter.5.cloned.1.call-update) | async-done | bytes 32784 | tf_op jit(solution)/shard_map/reduce_scatter | solution.py:50
  165.4 1.4 fusion.33
  (58 shorter events, 4.3 us)
Async XLA Ops:
  7.2 58.4 %copy-start = (bf16[48,2,128,128]{3,2,1,0:T(8,128)(2,1)S(1)}, bf16[48,2,128,128]{3,2,1,0:T(8,128)(2,1)}, u32[]{:S(2)}) copy-start(bf16[48,2,128,128]{3,2,1,0:T(8,128)(2,1)} %param.13) | copy-start | bytes 9437188
  7.2 82.3 %reduce-scatter.3.cloned.1.call-start = ((), (), s32[]{:S(2)}) async-start(), calls=%async_computation.2 | async-start | bytes 163840 | tf_op jit(solution)/shard_map/reduce_scatter | solution.py:50
  14.0 48.3 %copy-start.1 = (bf16[2,16,2048]{2,1,0:T(8,128)(2,1)}, bf16[2,16,2048]{2,1,0:T(8,128)(2,1)S(1)}, u32[]{:S(2)}) copy-start(bf16[2,16,2048]{2,1,0:T(8,128)(2,1)S(1)} %all_gather.12) | copy-start | bytes 393220
  14.1 48.3 %collective-permute-start = (bf16[2,16,2048]{2,1,0:T(8,128)(2,1)S(1)}, bf16[2,16,2048]{2,1,0:T(8,128)(2,1)S(1)}, u32[]{:S(2)}, u32[]{:S(2)}) collective-permute-start(bf16[2,16,2048]{2,1,0:T(8,128)(2,1)S(1)} %all_gather.12), channel_id=1, source_target_pairs={{0,4},{4,8},{8,12},{1,5},{5,9},{9,13},{2,6},{6,10},{10,14},{3,7},{... | collective-permute-start | bytes 393224 | tf_op jit(solution)/shard_map/ppermute | solution.py:12
  17.9 45.1 %collective-permute-start.1 = (bf16[2,16,2048]{2,1,0:T(8,128)(2,1)S(1)}, bf16[2,16,2048]{2,1,0:T(8,128)(2,1)}, u32[]{:S(2)}, u32[]{:S(2)}) collective-permute-start(bf16[2,16,2048]{2,1,0:T(8,128)(2,1)S(1)} %all_gather.12), channel_id=1, source_target_pairs={{4,0},{8,4},{12,8},{5,1},{9,5},{13,9},{6,2},{10,6},{14,10},{7,3},{... | collective-permute-start | bytes 393224 | tf_op jit(solution)/shard_map/ppermute | solution.py:15
  21.6 40.8 %copy-start.9 = (pred[8]{0:T(512)(128)(4,1)}, pred[8]{0:T(512)(128)(4,1)S(1)}, u32[]{:S(2)}) copy-start(pred[8]{0:T(512)(128)(4,1)S(1)} %compare_and_fusion) | copy-start | bytes 28
  62.4 0.7 copy-start.8
  67.8 1.5 copy-start.2
  67.9 33.2 %copy-start.7 = (bf16[2,32,512]{2,1,0:T(8,128)(2,1)S(1)}, bf16[2,32,512]{2,1,0:T(8,128)(2,1)}, u32[]{:S(2)}) copy-start(bf16[2,32,512]{2,1,0:T(8,128)(2,1)} %param.17) | copy-start | bytes 196612
  67.9 69.5 %copy-start.6 = (bf16[2,32,512]{2,1,0:T(8,128)(2,1)S(1)}, bf16[2,32,512]{2,1,0:T(8,128)(2,1)}, u32[]{:S(2)}) copy-start(bf16[2,32,512]{2,1,0:T(8,128)(2,1)} %param.16) | copy-start | bytes 196612
  69.2 96.2 %reduce-scatter.5.cloned.1.call-start = ((), (), s32[]{:S(2)}) async-start(), calls=%async_computation.3 | async-start | bytes 163840 | tf_op jit(solution)/shard_map/reduce_scatter | solution.py:50
  90.3 10.8 %copy-start.5 = (bf16[2,16,512]{2,1,0:T(8,128)(2,1)}, bf16[2,16,512]{2,1,0:T(8,128)(2,1)S(1)}, u32[]{:S(2)}) copy-start(bf16[2,16,512]{2,1,0:T(8,128)(2,1)S(1)} %fusion.32) | copy-start | bytes 98308
  95.7 42.5 %copy-start.3 = (bf16[2,16,2048]{2,1,0:T(8,128)(2,1)}, bf16[2,16,2048]{2,1,0:T(8,128)(2,1)S(1)}, u32[]{:S(2)}) copy-start(bf16[2,16,2048]{2,1,0:T(8,128)(2,1)S(1)} %all_gather.14) | copy-start | bytes 393220
  95.7 42.4 %collective-permute-start.2 = (bf16[2,16,2048]{2,1,0:T(8,128)(2,1)S(1)}, bf16[2,16,2048]{2,1,0:T(8,128)(2,1)}, u32[]{:S(2)}, u32[]{:S(2)}) collective-permute-start(bf16[2,16,2048]{2,1,0:T(8,128)(2,1)S(1)} %all_gather.14), channel_id=1, source_target_pairs={{0,4},{4,8},{8,12},{1,5},{5,9},{9,13},{2,6},{6,10},{10,14},{3,7},{... | collective-permute-start | bytes 393224 | tf_op jit(solution)/shard_map/ppermute | solution.py:12
  99.8 38.4 %collective-permute-start.3 = (bf16[2,16,2048]{2,1,0:T(8,128)(2,1)S(1)}, bf16[2,16,2048]{2,1,0:T(8,128)(2,1)}, u32[]{:S(2)}, u32[]{:S(2)}) collective-permute-start(bf16[2,16,2048]{2,1,0:T(8,128)(2,1)S(1)} %all_gather.14), channel_id=1, source_target_pairs={{4,0},{8,4},{12,8},{5,1},{9,5},{13,9},{6,2},{10,6},{14,10},{7,3},{... | collective-permute-start | bytes 393224 | tf_op jit(solution)/shard_map/ppermute | solution.py:15
  143.0 1.4 copy-start.4
Sparse Core Ops, SparseCore 0:
  69.4 20.1 reduce-scatter.2
  144.5 20.9 reduce-scatter.4
where the time goes:
time: 174 us
  blocking collectives  82.6 us (47%)
  waiting for transfers between devices  41.3 us (24%)
  between operations  14.4 us (8%)
  matrix products  11.4 us (7%)
  starting transfers between devices  10.6 us (6%)
  other arithmetic  7.42 us (4%)
  local copies, waits for them, and re-layouts  5.99 us (3%)
    reduce_scatter x2, waiting for transfers between devices, apply_operator(): lax.psum_scatter(spread.reshape(2, rhs_count, sub_rows).astype(jnp.bfloat...  41.2 us
    all_gather x2, blocking collectives, apply_operator(): lax.all_gather(summed.astype(jnp.bfloat16)[None], 'clus', axis=0, tiled=T...  28.1 us
    psum x2, blocking collectives, apply_operator(): summed = lax.psum(partial_value, 'sub')  21.8 us
    psum x2, blocking collectives, apply_operator(): coupled = lax.psum(coupled_terms, 'sub').astype(jnp.bfloat16)  20.4 us
    all_gather x2, blocking collectives, apply_operator(): subtree = lax.all_gather(current, 'sub', axis=2, tiled=True)  12.3 us
    ppermute x2, starting transfers between devices, padded(): lax.ppermute(lax.slice_in_dim(block, block.shape[dim] - width, None, axis...  7.9 us
    dot_general x2, matrix products, apply_operator(): jnp.einsum('bqrc,pnbc->qpnbr', near_blocks, picked, preferred_element_typ...  4.36 us
  transfers between devices with their start and end apart: 6, of which 2 were waited for; matrix products, arithmetic and copies ran while one was open for 6% of the time, Pallas kernels for 0%

commit v1 on v0

v1 whole, which is shorter than its diff:
```python
import functools

import jax
import jax.numpy as jnp
from jax import lax
from jax.experimental import pallas as pl
from jax.experimental.pallas import tpu as pltpu
from jax.sharding import PartitionSpec as P

F32 = jnp.float32
BF16 = jnp.bfloat16
NT = (((1,), (1,)), ((), ()))
CHUNKS = 4
STEP = 8


def kernel(
    clus_count, sub_count, leaf_size,
    vec, blocks, rows, cols, rowb, colb, coup, farc,
    out0, out1,
    blk, blk_sem, idx_v, idx_s, idx_sem, wcol, wcoup, xw0, xw1, xrs, xss, fss,
    csend, crecv, crs, css, coef0, coef1, grs, gss,
    dsend, drecv, drs, dss, sums, nown, nsend, nrecv, nrs, nss,
):
    t = lax.axis_index("clus")
    s = lax.axis_index("sub")
    g = s // 2
    c = s - 2 * g
    groups = sub_count // 2
    leaf_dev = vec.shape[2] // leaf_size
    sub_leaves = leaf_dev * sub_count
    rhs = vec.shape[1]
    nb = blk.shape[0]
    part = nb // CHUNKS
    far_dev = coup.shape[0]
    partner = 2 * g + 1 - c

    loads = [
        pltpu.make_async_copy(
            blocks.at[pl.ds(i * part, part)], blk.at[pl.ds(i * part, part)], blk_sem.at[i]
        )
        for i in range(CHUNKS)
    ]
    for load in loads:
        load.start()

    def has(dt):
        return (t > 0) if dt < 0 else (t < clus_count - 1)

    def remote(src, dst, ssem, rsem, tt, ss):
        return pltpu.make_async_remote_copy(
            src_ref=src, dst_ref=dst, send_sem=ssem, recv_sem=rsem,
            device_id={"clus": tt, "sub": ss}, device_id_type=pl.DeviceIdType.MESH,
        )

    barrier = pltpu.get_barrier_semaphore()

    def greet(tt, ss):
        pl.semaphore_signal(
            barrier, inc=1, device_id={"clus": tt, "sub": ss}, device_id_type=pl.DeviceIdType.MESH
        )

    for j in range(1, sub_count):
        greet(t, lax.rem(s + j, sub_count))
    expected = sub_count - 1
    for dt in (-1, 1):
        @pl.when(has(dt))
        def _(dt=dt):
            for j in range(groups):
                greet(t + dt, 2 * lax.rem(g + j, groups) + c)

        expected = expected + jnp.where(has(dt), groups, 0)
    for d in range(2, clus_count):
        for sign in (-1, 1):
            ok = (t - d >= 0) if sign < 0 else (t + d < clus_count)

            @pl.when(ok)
            def _(d=d, sign=sign):
                greet(t + sign * d, s)

            expected = expected + jnp.where(ok, 1, 0)

    i0 = lax.broadcasted_iota(jnp.int32, (nb, nb), 0)
    i1 = lax.broadcasted_iota(jnp.int32, (nb, nb), 1)
    row_l = jnp.clip(rows[...] - t * sub_leaves, 0, sub_leaves - 1)
    col_l = jnp.clip(cols[...] - (t - 1) * sub_leaves, 0, 3 * sub_leaves - 1)
    eye = i0 == i1
    row_c = jnp.sum(jnp.where(eye, row_l, 0), axis=1, keepdims=True)
    col_c = jnp.sum(jnp.where(eye, col_l, 0), axis=1, keepdims=True)
    key_r = row_l * nb + i1
    key_c = row_c * nb + i0
    rank = jnp.sum(jnp.where(key_r < key_c, 1, 0), axis=1, keepdims=True)
    hit = rank == i1
    idx_v[0:1, 0:nb] = jnp.sum(jnp.where(hit, i0, 0), axis=0, keepdims=True)
    idx_v[1:2, 0:nb] = jnp.sum(jnp.where(hit, row_c, 0), axis=0, keepdims=True)
    idx_v[2:3, 0:nb] = jnp.sum(jnp.where(hit, col_c, 0), axis=0, keepdims=True)
    leaf = lax.broadcasted_iota(jnp.int32, (nb, sub_leaves), 1)
    upto = jnp.sum(jnp.where(row_c <= leaf, 1, 0), axis=0, keepdims=True)
    here = jnp.sum(jnp.where(row_c == leaf, 1, 0), axis=0, keepdims=True)
    idx_v[3:4, 0:sub_leaves] = jnp.where(here > 0, upto, 0)
    idx_copy = pltpu.make_async_copy(idx_v, idx_s, idx_sem)
    idx_copy.start()

    wcol[...] = jnp.concatenate(
        [
            jnp.concatenate([colb[0], -colb[1]], axis=1),
            jnp.concatenate([colb[1], colb[0]], axis=1),
        ],
        axis=0,
    )

    def slot(w, ss):
        return pl.ds((w * sub_count + ss) * leaf_dev, leaf_dev)

    own = (sub_count + s) * leaf_dev
    for l in range(leaf_dev):
        for p in range(2):
            xw0[own + l, p] = vec[p, :, l * leaf_size : (l + 1) * leaf_size]
    sums[0] = jnp.zeros(sums.shape[1:], F32)

    pl.semaphore_wait(barrier, expected)

    for prod in range(2):
        x = vec if prod == 0 else out0
        out = out0 if prod == 0 else out1
        xw = (xw0, xw1)[prod]
        coef = (coef0, coef1)[prod]

        def shard_send(dt, j, prod=prod, xw=xw):
            target = partner if (dt == 0 and j == 0) else 2 * lax.rem(g + j, groups) + c
            return remote(
                xw.at[slot(1, s)], xw.at[slot(1 - dt, s)],
                xss.at[prod, dt + 1, j], xrs.at[prod, 1 - dt, s], t + dt, target,
            )

        def forward(w, j, prod=prod, xw=xw):
            ss = 2 * lax.rem(g + j, groups) + c
            return remote(
                xw.at[slot(w, ss)], xw.at[slot(w, ss)],
                fss.at[prod, w, j], xrs.at[prod, w, ss], t, partner,
            )

        def from_partner(w, j, prod=prod, xw=xw):
            ss = 2 * lax.rem(g + j, groups) + 1 - c
            return remote(
                xw.at[slot(w, ss)], xw.at[slot(w, ss)],
                fss.at[prod, w, j], xrs.at[prod, w, ss], t, partner,
            )

        for j in list(range(1, groups)) + [0]:
            for dt in (-1, 1):
                @pl.when(has(dt))
                def _(dt=dt, j=j):
                    shard_send(dt, j).start()
            shard_send(0, j).start()

        lhs = jnp.concatenate([x[0], x[1]], axis=1)
        partial = lax.dot_general(lhs, wcol[...], NT, preferred_element_type=F32)
        csend[prod] = partial

        def coef_send(j, prod=prod):
            return remote(
                csend.at[prod], crecv.at[prod, s], css.at[prod, j], crs.at[prod, s],
                t, lax.rem(s + j, sub_count),
            )

        def coef_recv(j, prod=prod):
            ss = lax.rem(s + j, sub_count)
            return remote(
                csend.at[prod], crecv.at[prod, ss], css.at[prod, j], crs.at[prod, ss], t, ss
            )

        for j in range(1, sub_count):
            coef_send(j).start()
        if prod == 0:
            for f in range(far_dev):
                wcoup[f] = jnp.concatenate(
                    [
                        jnp.concatenate([coup[f, 0], -coup[f, 1]], axis=1),
                        jnp.concatenate([coup[f, 1], coup[f, 0]], axis=1),
                    ],
                    axis=0,
                )
        for j in range(1, sub_count):
            coef_recv(j).wait_recv()
            partial = partial + crecv[prod, lax.rem(s + j, sub_count)]
        coef[t] = partial.astype(BF16)

        def gather_send(d, prod=prod, coef=coef):
            return remote(
                coef.at[t], coef.at[t], gss.at[prod, d], grs.at[prod, t],
                lax.rem(t + d, clus_count), s,
            )

        def gather_recv(d, prod=prod, coef=coef):
            tt = lax.rem(t + d, clus_count)
            return remote(coef.at[tt], coef.at[tt], gss.at[prod, d], grs.at[prod, tt], tt, s)

        for d in range(1, clus_count):
            gather_send(d).start()

        for j in range(groups):
            for dt in (-1, 1):
                @pl.when(has(dt))
                def _(dt=dt, j=j):
                    hop = forward(1 + dt, j)
                    hop.wait_recv()
                    hop.start()
            if j > 0:
                hop = forward(1, j)
                hop.wait_recv()
                hop.start()

        for d in range(1, clus_count):
            gather_recv(d).wait_recv()
        coupled = jnp.zeros(partial.shape, F32)
        for f in range(far_dev):
            coupled = coupled + lax.dot_general(
                coef[farc[f]], wcoup[f], NT, preferred_element_type=F32
            )
        dsend[prod] = coupled

        def coupled_send(j, prod=prod):
            return remote(
                dsend.at[prod], drecv.at[prod, s], dss.at[prod, j], drs.at[prod, s],
                t, lax.rem(s + j, sub_count),
            )

        def coupled_recv(j, prod=prod):
            ss = lax.rem(s + j, sub_count)
            return remote(
                dsend.at[prod], drecv.at[prod, ss], dss.at[prod, j], drs.at[prod, ss], t, ss
            )

        for j in range(1, sub_count):
            coupled_send(j).start()

        if prod == 0:
            idx_copy.wait()
            for load in loads:
                load.wait()
        for j in range(groups):
            for dt in (-1, 1):
                @pl.when(has(dt))
                def _(dt=dt, j=j):
                    from_partner(1 + dt, j).wait_recv()
            from_partner(1, j).wait_recv()

        def body(i, total, xw=xw):
            for u in range(STEP):
                k = i * STEP + u
                a = blk[idx_s[0, k]]
                v = xw[idx_s[2, k]]
                left = jnp.concatenate(
                    [
                        jnp.concatenate([v[0], -v[1]], axis=1),
                        jnp.concatenate([v[1], v[0]], axis=1),
                    ],
                    axis=0,
                )
                term = lax.dot_general(
                    left, jnp.concatenate([a[0], a[1]], axis=1), NT, preferred_element_type=F32
                )
                same = idx_s[1, k] == idx_s[1, jnp.maximum(k - 1, 0)]
                total = jnp.where(same, total, 0.0) + term
                sums[k + 1] = total
            return total

        lax.fori_loop(0, nb // STEP, body, jnp.zeros(sums.shape[1:], F32))

        def near_send(jg, e, prod=prod):
            ss = 2 * lax.rem(g + jg, groups) + lax.rem(c + e, 2)
            return ss, remote(
                nsend.at[prod, ss], nrecv.at[prod, s], nss.at[prod, jg, e], nrs.at[prod, s], t, ss
            )

        def near_recv(jg, e, prod=prod):
            ss = 2 * lax.rem(g + jg, groups) + lax.rem(c + e, 2)
            return ss, remote(
                nsend.at[prod, ss], nrecv.at[prod, ss], nss.at[prod, jg, e], nrs.at[prod, ss], t, ss
            )

        others = [(jg, e) for jg in list(range(1, groups)) + [0] for e in range(2)]
        others.remove((0, 0))
        for jg, e in others:
            ss, copy = near_send(jg, e)
            for l in range(leaf_dev):
                nsend[prod, ss, l] = sums[idx_s[3, ss * leaf_dev + l]].astype(BF16)
            copy.start()

        coupled = dsend[prod]
        for j in range(1, sub_count):
            coupled_recv(j).wait_recv()
            coupled = coupled + drecv[prod, lax.rem(s + j, sub_count)]
        coupled = coupled.astype(BF16)
        rank_size = coupled.shape[1] // 2
        c0, c1 = coupled[:, :rank_size], coupled[:, rank_size:]
        left = jnp.concatenate(
            [jnp.concatenate([c0, -c1], axis=1), jnp.concatenate([c1, c0], axis=1)], axis=0
        )
        right = jnp.concatenate([rowb[0], rowb[1]], axis=0)
        far = jnp.dot(left, right, preferred_element_type=F32)
        for l in range(leaf_dev):
            nown[l] = far[:, l * leaf_size : (l + 1) * leaf_size] + sums[
                idx_s[3, s * leaf_dev + l]
            ].astype(BF16).astype(F32)

        for jg, e in others[::-1]:
            near_recv(jg, e)[1].wait_recv()
        for l in range(leaf_dev):
            total = nown[l]
            for jg, e in others:
                ss = 2 * lax.rem(g + jg, groups) + lax.rem(c + e, 2)
                total = total + nrecv[prod, ss, l].astype(F32)
            total = total.astype(BF16)
            for p in range(2):
                piece = total[p * rhs : (p + 1) * rhs]
                out[p, :, l * leaf_size : (l + 1) * leaf_size] = piece
                if prod == 0:
                    xw1[own + l, p] = piece

    for prod in range(2):
        xw = (xw0, xw1)[prod]
        coef = (coef0, coef1)[prod]

        def sent(src, sem):
            remote(src, src, sem, sem, t, partner).wait_send()

        for j in range(groups):
            for dt in (-1, 1):
                @pl.when(has(dt))
                def _(dt=dt, j=j, prod=prod, xw=xw):
                    sent(xw.at[slot(1, s)], xss.at[prod, dt + 1, j])
                    ss = 2 * lax.rem(g + j, groups) + c
                    sent(xw.at[slot(1 + dt, ss)], fss.at[prod, 1 + dt, j])
            sent(xw.at[slot(1, s)], xss.at[prod, 1, j])
            if j > 0:
                ss = 2 * lax.rem(g + j, groups) + c
                sent(xw.at[slot(1, ss)], fss.at[prod, 1, j])
        for j in range(1, sub_count):
            sent(csend.at[prod], css.at[prod, j])
            sent(dsend.at[prod], dss.at[prod, j])
        for d in range(1, clus_count):
            sent(coef.at[t], gss.at[prod, d])
        for jg in range(groups):
            for e in range(2):
                if (jg, e) != (0, 0):
                    ss = 2 * lax.rem(g + jg, groups) + lax.rem(c + e, 2)
                    sent(nsend.at[prod, ss], nss.at[prod, jg, e])


def per_device(
    vector, near_blocks, near_rows, near_cols, row_basis, col_basis, couplings, far_cols
):
    sub_count = lax.axis_size("sub")
    clus_count = lax.axis_size("clus")
    groups = sub_count // 2
    nb, _, leaf_size, _ = near_blocks.shape
    _, rhs, rows_dev = vector.shape
    leaf_dev = rows_dev // leaf_size
    window = 3 * sub_count * leaf_dev
    rank = row_basis.shape[1]
    far_dev = couplings.shape[0]
    dma = pltpu.SemaphoreType.DMA
    small = (rhs, 2 * rank)
    vmem = pl.BlockSpec(memory_space=pltpu.VMEM)
    smem = pl.BlockSpec(memory_space=pltpu.SMEM)
    return pl.pallas_call(
        functools.partial(kernel, clus_count, sub_count, leaf_size),
        out_shape=(
            jax.ShapeDtypeStruct(vector.shape, BF16),
            jax.ShapeDtypeStruct(vector.shape, BF16),
        ),
        in_specs=[vmem, pl.BlockSpec(memory_space=pl.ANY), vmem, vmem, vmem, vmem, vmem, smem],
        out_specs=(vmem, vmem),
        scratch_shapes=[
            pltpu.VMEM(near_blocks.shape, BF16), dma((CHUNKS,)),
            pltpu.VMEM((8, 128), jnp.int32), pltpu.SMEM((8, 128), jnp.int32), dma(()),
            pltpu.VMEM((2 * rank, 2 * rows_dev), BF16),
            pltpu.VMEM((far_dev, 2 * rank, 2 * rank), BF16),
            pltpu.VMEM((window, 2, rhs, leaf_size), BF16),
            pltpu.VMEM((window, 2, rhs, leaf_size), BF16),
            dma((2, 3, sub_count)), dma((2, 3, groups)), dma((2, 3, groups)),
            pltpu.VMEM((2,) + small, F32), pltpu.VMEM((2, sub_count) + small, F32),
            dma((2, sub_count)), dma((2, sub_count)),
            pltpu.VMEM((clus_count,) + small, BF16), pltpu.VMEM((clus_count,) + small, BF16),
            dma((2, clus_count)), dma((2, clus_count)),
            pltpu.VMEM((2,) + small, F32), pltpu.VMEM((2, sub_count) + small, F32),
            dma((2, sub_count)), dma((2, sub_count)),
            pltpu.VMEM((nb + 1, 2 * rhs, leaf_size), F32),
            pltpu.VMEM((leaf_dev, 2 * rhs, leaf_size), F32),
            pltpu.VMEM((2, sub_count, leaf_dev, 2 * rhs, leaf_size), BF16),
            pltpu.VMEM((2, sub_count, leaf_dev, 2 * rhs, leaf_size), BF16),
            dma((2, sub_count)), dma((2, groups, 2)),
        ],
        compiler_params=pltpu.CompilerParams(
            collective_id=0, has_side_effects=True, vmem_limit_bytes=40 * 1024 * 1024
        ),
        name="operator",
    )(
        vector, near_blocks, near_rows.reshape(1, nb), near_cols.reshape(1, nb),
        row_basis, col_basis, couplings, far_cols,
    )


def solution(mesh):
    in_specs = (
        P(None, None, ("parts", "clus", "sub")),
        P(("parts", "clus", "sub"), None, None, None),
        P(("parts", "clus", "sub")),
        P(("parts", "clus", "sub")),
        P(None, None, ("parts", "clus", "sub")),
        P(None, None, ("parts", "clus", "sub")),
        P(("parts", "clus", "sub"), None, None, None),
        P(("parts", "clus", "sub")),
    )
    out_specs = (P(None, None, ("parts", "clus", "sub")), P(None, None, ("parts", "clus", "sub")))
    return jax.shard_map(
        per_device, mesh=mesh, in_specs=in_specs, out_specs=out_specs, check_vma=False
    )
```

time: 174 us -> 40.3 us (0.23)
  blocking collectives: 82.6 us -> 0 us
  waiting for transfers between devices: 41.3 us -> 0 us
  Pallas kernels: 0 us -> 30.8 us
  between operations: 14.4 us -> 0.66 us
  matrix products: 11.4 us -> 0 us
  starting transfers between devices: 10.6 us -> 0 us
  other arithmetic: 7.42 us -> 0 us
  local copies, waits for them, and re-layouts: 5.99 us -> 8.42 us
    psum x4 -> x0, blocking collectives: 42.2 us -> none  [the longest x2 21.8 us: apply_operator(): summed = lax.psum(partial_value, 'sub')]
    reduce_scatter x2 -> x0, waiting for transfers between devices: 41.2 us -> none  [apply_operator(): lax.psum_scatter(spread.reshape(2, rhs_count, sub_rows).astype(jnp.bfloat...]
    all_gather x4 -> x0, blocking collectives: 40.4 us -> none  [the longest x2 28.1 us: apply_operator(): lax.all_gather(summed.astype(jnp.bfloat16)[None], 'clus', axis=0, tiled=T...]
    pallas_call x0 -> x1, Pallas kernels: none -> 30.8 us  [per_device(): pl.pallas_call(functools.partial(kernel, clus_count, sub_count, leaf_size...]
    dot_general x10 -> x0, matrix products: 11.4 us -> none  [the longest x2 4.36 us: apply_operator(): jnp.einsum('bqrc,pnbc->qpnbr', near_blocks, picked, preferred_element_typ...]
    ppermute x4 -> x0, starting transfers between devices: 10.5 us -> none  [the longest x2 7.9 us: padded(): lax.ppermute(lax.slice_in_dim(block, block.shape[dim] - width, None, axis...]
    unnamed x20 -> x18, local copies, waits for them, and re-layouts: 0.69 us -> 8.42 us
    gather x4 -> x0, local copies, waits for them, and re-layouts: 3.89 us -> none  [the longest x2 2.76 us: apply_operator(): picked = jnp.take(pieces, col_local, axis=2)]
  transfers between devices with their start and end apart: 6 -> 0, of which waited for: 2 -> 0; matrix products, arithmetic and copies ran while one was open for 6% -> 0% of each run, Pallas kernels for 0% -> 0%
where the time goes in v1:
time: 40.3 us; the launch traced here: 39.9 us
  Pallas kernels  30.8 us (76%)
  local copies, waits for them, and re-layouts  8.42 us (21%)
  between operations  0.66 us (2%)
    pallas_call x1, Pallas kernels, per_device(): pl.pallas_call(functools.partial(kernel, clus_count, sub_count, leaf_size...  30.8 us
    unnamed x18, local copies, waits for them, and re-layouts  8.42 us

profile of v1, /device:TPU:0, one launch (start us, length us, event | category | flops | bytes accessed | tf_op | source)
XLA Modules:
  0.0 39.9 jit_solution(17621489398119653247)
XLA Ops:
  0.6 0.0 copy-start
  0.6 1.9 %copy-done = bf16[48,2,128,128]{3,2,1,0:T(8,128)(2,1)S(1)} copy-done((bf16[48,2,128,128]{3,2,1,0:T(8,128)(2,1)S(1)}, bf16[48,2,128,128]{3,2,1,0:T(8,128)(2,1)}, u32[]{:S(2)}) %copy-start) | copy-done | bytes 3145752
  2.5 0.0 copy-start.1
  2.5 0.9 %copy-done.1 = bf16[8,2,32,32]{3,2,1,0:T(8,128)(2,1)S(1)} copy-done((bf16[8,2,32,32]{3,2,1,0:T(8,128)(2,1)S(1)}, bf16[8,2,32,32]{3,2,1,0:T(8,128)(2,1)}, u32[]{:S(2)}) %copy-start.1) | copy-done | bytes 32792
  3.4 0.0 copy-start.2
  3.4 0.8 %copy-done.2 = bf16[2,32,512]{2,1,0:T(8,128)(2,1)S(1)} copy-done((bf16[2,32,512]{2,1,0:T(8,128)(2,1)S(1)}, bf16[2,32,512]{2,1,0:T(8,128)(2,1)}, u32[]{:S(2)}) %copy-start.2) | copy-done | bytes 65560
  4.3 0.0 copy-start.3
  4.3 0.8 %copy-done.3 = bf16[2,32,512]{2,1,0:T(8,128)(2,1)S(1)} copy-done((bf16[2,32,512]{2,1,0:T(8,128)(2,1)S(1)}, bf16[2,32,512]{2,1,0:T(8,128)(2,1)}, u32[]{:S(2)}) %copy-start.3) | copy-done | bytes 65560
  5.1 0.0 copy-start.4
  5.1 0.8 %copy-done.4 = bf16[2,16,512]{2,1,0:T(8,128)(2,1)S(1)} copy-done((bf16[2,16,512]{2,1,0:T(8,128)(2,1)S(1)}, bf16[2,16,512]{2,1,0:T(8,128)(2,1)}, u32[]{:S(2)}) %copy-start.4) | copy-done | bytes 32792
  5.9 0.0 copy-start.5
  5.9 0.7 %copy-done.5 = s32[48]{0:T(128)S(1)} copy-done((s32[48]{0:T(128)S(1)}, s32[48]{0:T(128)}, u32[]{:S(2)}) %copy-start.5) | copy-done | bytes 216
  6.5 0.0 copy-start.6
  6.5 0.7 %copy-done.6 = s32[48]{0:T(128)S(1)} copy-done((s32[48]{0:T(128)S(1)}, s32[48]{0:T(128)}, u32[]{:S(2)}) %copy-start.6) | copy-done | bytes 216
  7.2 0.0 copy-start.7
  7.2 0.7 %copy-done.7 = s32[8]{0:T(128)S(1)} copy-done((s32[8]{0:T(128)S(1)}, s32[8]{0:T(128)}, u32[]{:S(2)}) %copy-start.7) | copy-done | bytes 56
  7.8 30.8 %operator.1 = (bf16[2,16,512]{2,1,0:T(8,128)(2,1)S(1)}, bf16[2,16,512]{2,1,0:T(8,128)(2,1)S(1)}) custom-call(bf16[2,16,512]{2,1,0:T(8,128)(2,1)S(1)} %copy-done.4, bf16[48,2,128,128]{3,2,1,0:T(8,128)(2,1)S(1)} %copy-done, s32[1,48]{1,0:T(1,128)S(1)} %bitcast.2, s32[1,48]{1,0:T(1,128)S(1)} %bitcast.3, bf16[2,32,512]{2,1,0:T(8,128)(2,1)S(1)} %copy-done.2, ...), custom_call_target="tpu_custom_call" | custom-call | tf_op jit(solution)/shard_map/operator/pallas_call | solution.py:368
  38.7 0.6 %copy.12 = bf16[2,16,512]{2,1,0:T(8,128)(2,1)} copy(bf16[2,16,512]{2,1,0:T(8,128)(2,1)S(1)} %get-tuple-element.4) | data formatting | bytes 65536
  39.3 0.6 %copy.13 = bf16[2,16,512]{2,1,0:T(8,128)(2,1)} copy(bf16[2,16,512]{2,1,0:T(8,128)(2,1)S(1)} %get-tuple-element.5) | data formatting | bytes 65536
Async XLA Ops:
  0.6 1.9 %copy-start = (bf16[48,2,128,128]{3,2,1,0:T(8,128)(2,1)S(1)}, bf16[48,2,128,128]{3,2,1,0:T(8,128)(2,1)}, u32[]{:S(2)}) copy-start(bf16[48,2,128,128]{3,2,1,0:T(8,128)(2,1)} %blocks.1) | copy-start | bytes 9437188
  2.5 0.9 %copy-start.1 = (bf16[8,2,32,32]{3,2,1,0:T(8,128)(2,1)S(1)}, bf16[8,2,32,32]{3,2,1,0:T(8,128)(2,1)}, u32[]{:S(2)}) copy-start(bf16[8,2,32,32]{3,2,1,0:T(8,128)(2,1)} %coup.1) | copy-start | bytes 98308
  3.4 0.8 %copy-start.2 = (bf16[2,32,512]{2,1,0:T(8,128)(2,1)S(1)}, bf16[2,32,512]{2,1,0:T(8,128)(2,1)}, u32[]{:S(2)}) copy-start(bf16[2,32,512]{2,1,0:T(8,128)(2,1)} %rowb.1) | copy-start | bytes 196612
  4.3 0.8 %copy-start.3 = (bf16[2,32,512]{2,1,0:T(8,128)(2,1)S(1)}, bf16[2,32,512]{2,1,0:T(8,128)(2,1)}, u32[]{:S(2)}) copy-start(bf16[2,32,512]{2,1,0:T(8,128)(2,1)} %colb.1) | copy-start | bytes 196612
  5.1 0.8 %copy-start.4 = (bf16[2,16,512]{2,1,0:T(8,128)(2,1)S(1)}, bf16[2,16,512]{2,1,0:T(8,128)(2,1)}, u32[]{:S(2)}) copy-start(bf16[2,16,512]{2,1,0:T(8,128)(2,1)} %vec.1) | copy-start | bytes 98308
  5.9 0.7 %copy-start.5 = (s32[48]{0:T(128)S(1)}, s32[48]{0:T(128)}, u32[]{:S(2)}) copy-start(s32[48]{0:T(128)} %param.10) | copy-start | bytes 580
  6.5 0.7 %copy-start.6 = (s32[48]{0:T(128)S(1)}, s32[48]{0:T(128)}, u32[]{:S(2)}) copy-start(s32[48]{0:T(128)} %param.11) | copy-start | bytes 580
  7.2 0.7 %copy-start.7 = (s32[8]{0:T(128)S(1)}, s32[8]{0:T(128)}, u32[]{:S(2)}) copy-start(s32[8]{0:T(128)} %farc.1) | copy-start | bytes 100

commit v2 on v1

--- a/solution.py
+++ b/solution.py
@@ -11,13 +11,14 @@
 BF16 = jnp.bfloat16
 NT = (((1,), (1,)), ((), ()))
 CHUNKS = 4
-STEP = 8
+STEP = 48
 
 
 def kernel(
     clus_count, sub_count, leaf_size,
-    vec, blocks, rows, cols, rowb, colb, coup, farc,
+    vec_h, blocks, rows_h, cols_h, rowb_h, colb_h, coup_h, farc_h,
     out0, out1,
+    vec, rows, cols, rowb, colb, coup, farc, in_sem,
     blk, blk_sem, idx_v, idx_s, idx_sem, wcol, wcoup, xw0, xw1, xrs, xss, fss,
     csend, crecv, crs, css, coef0, coef1, grs, gss,
     dsend, drecv, drs, dss, sums, nown, nsend, nrecv, nrs, nss,
@@ -35,6 +36,17 @@
     far_dev = coup.shape[0]
     partner = 2 * g + 1 - c
 
+    vec_in, rows_in, cols_in, farc_in, colb_in, coup_in, rowb_in = [
+        pltpu.make_async_copy(source, target, in_sem.at[i])
+        for i, (source, target) in enumerate(
+            [
+                (vec_h, vec), (rows_h, rows), (cols_h, cols), (farc_h, farc),
+                (colb_h, colb), (coup_h, coup), (rowb_h, rowb),
+            ]
+        )
+    ]
+    for load in (vec_in, rows_in, cols_in, farc_in, colb_in, coup_in, rowb_in):
+        load.start()
     loads = [
         pltpu.make_async_copy(
             blocks.at[pl.ds(i * part, part)], blk.at[pl.ds(i * part, part)], blk_sem.at[i]
@@ -79,6 +91,18 @@
                 greet(t + sign * d, s)
 
             expected = expected + jnp.where(ok, 1, 0)
+
+    def slot(w, ss):
+        return pl.ds((w * sub_count + ss) * leaf_dev, leaf_dev)
+
+    own = (sub_count + s) * leaf_dev
+    vec_in.wait()
+    for l in range(leaf_dev):
+        for p in range(2):
+            xw0[own + l, p] = vec[p, :, l * leaf_size : (l + 1) * leaf_size]
+    sums[0] = jnp.zeros(sums.shape[1:], F32)
+    for load in (rows_in, cols_in, farc_in):
+        load.wait()
 
     i0 = lax.broadcasted_iota(jnp.int32, (nb, nb), 0)
     i1 = lax.broadcasted_iota(jnp.int32, (nb, nb), 1)
@@ -98,9 +122,11 @@
     upto = jnp.sum(jnp.where(row_c <= leaf, 1, 0), axis=0, keepdims=True)
     here = jnp.sum(jnp.where(row_c == leaf, 1, 0), axis=0, keepdims=True)
     idx_v[3:4, 0:sub_leaves] = jnp.where(here > 0, upto, 0)
+    idx_v[4:5, 0:far_dev] = farc[...]
     idx_copy = pltpu.make_async_copy(idx_v, idx_s, idx_sem)
     idx_copy.start()
 
+    colb_in.wait()
     wcol[...] = jnp.concatenate(
         [
             jnp.concatenate([colb[0], -colb[1]], axis=1),
@@ -109,15 +135,6 @@
         axis=0,
     )
 
-    def slot(w, ss):
-        return pl.ds((w * sub_count + ss) * leaf_dev, leaf_dev)
-
-    own = (sub_count + s) * leaf_dev
-    for l in range(leaf_dev):
-        for p in range(2):
-            xw0[own + l, p] = vec[p, :, l * leaf_size : (l + 1) * leaf_size]
-    sums[0] = jnp.zeros(sums.shape[1:], F32)
-
     pl.semaphore_wait(barrier, expected)
 
     for prod in range(2):
@@ -173,6 +190,9 @@
         for j in range(1, sub_count):
             coef_send(j).start()
         if prod == 0:
+            coup_in.wait()
+            rowb_in.wait()
+            idx_copy.wait()
             for f in range(far_dev):
                 wcoup[f] = jnp.concatenate(
                     [
@@ -216,7 +236,7 @@
         coupled = jnp.zeros(partial.shape, F32)
         for f in range(far_dev):
             coupled = coupled + lax.dot_general(
-                coef[farc[f]], wcoup[f], NT, preferred_element_type=F32
+                coef[idx_s[4, f]], wcoup[f], NT, preferred_element_type=F32
             )
         dsend[prod] = coupled
 
@@ -236,7 +256,6 @@
             coupled_send(j).start()
 
         if prod == 0:
-            idx_copy.wait()
             for load in loads:
                 load.wait()
         for j in range(groups):
@@ -364,16 +383,19 @@
     dma = pltpu.SemaphoreType.DMA
     small = (rhs, 2 * rank)
     vmem = pl.BlockSpec(memory_space=pltpu.VMEM)
-    smem = pl.BlockSpec(memory_space=pltpu.SMEM)
     return pl.pallas_call(
         functools.partial(kernel, clus_count, sub_count, leaf_size),
         out_shape=(
             jax.ShapeDtypeStruct(vector.shape, BF16),
             jax.ShapeDtypeStruct(vector.shape, BF16),
         ),
-        in_specs=[vmem, pl.BlockSpec(memory_space=pl.ANY), vmem, vmem, vmem, vmem, vmem, smem],
+        in_specs=[pl.BlockSpec(memory_space=pl.ANY)] * 8,
         out_specs=(vmem, vmem),
         scratch_shapes=[
+            pltpu.VMEM(vector.shape, BF16), pltpu.VMEM((1, nb), jnp.int32),
+            pltpu.VMEM((1, nb), jnp.int32), pltpu.VMEM(row_basis.shape, BF16),
+            pltpu.VMEM(col_basis.shape, BF16), pltpu.VMEM(couplings.shape, BF16),
+            pltpu.VMEM((1, far_dev), jnp.int32), dma((7,)),
             pltpu.VMEM(near_blocks.shape, BF16), dma((CHUNKS,)),
             pltpu.VMEM((8, 128), jnp.int32), pltpu.SMEM((8, 128), jnp.int32), dma(()),
             pltpu.VMEM((2 * rank, 2 * rows_dev), BF16),
@@ -394,12 +416,12 @@
             dma((2, sub_count)), dma((2, groups, 2)),
         ],
         compiler_params=pltpu.CompilerParams(
-            collective_id=0, has_side_effects=True, vmem_limit_bytes=40 * 1024 * 1024
+            collective_id=0, has_side_effects=True, vmem_limit_bytes=60 * 1024 * 1024
         ),
         name="operator",
     )(
         vector, near_blocks, near_rows.reshape(1, nb), near_cols.reshape(1, nb),
-        row_basis, col_basis, couplings, far_cols,
+        row_basis, col_basis, couplings, far_cols.reshape(1, far_dev),
     )
 
 

time: 40.3 us -> 33.1 us (0.82)
  local copies, waits for them, and re-layouts: 8.42 us -> 2.75 us
  Pallas kernels: 30.8 us -> 29.4 us
    unnamed x18 -> x2, local copies, waits for them, and re-layouts: 8.42 us -> 2.75 us
    pallas_call x1, Pallas kernels: 30.8 us -> 29.4 us  [per_device(): pl.pallas_call(functools.partial(kernel, clus_count, sub_count, leaf_size...]
where the time goes in v2:
time: 33.1 us; the launch traced here: 32.8 us
  Pallas kernels  29.4 us (89%)
  local copies, waits for them, and re-layouts  2.75 us (8%)
  between operations  0.64 us (2%)
    pallas_call x1, Pallas kernels, per_device(): pl.pallas_call(functools.partial(kernel, clus_count, sub_count, leaf_size...  29.4 us
    unnamed x2, local copies, waits for them, and re-layouts  2.75 us

profile of v2, /device:TPU:0, one launch (start us, length us, event | category | flops | bytes accessed | tf_op | source)
XLA Modules:
  0.0 32.8 jit_solution(3183185250630919359)
XLA Ops:
  0.6 29.4 %operator.1 = (bf16[2,16,512]{2,1,0:T(8,128)(2,1)}, bf16[2,16,512]{2,1,0:T(8,128)(2,1)}) custom-call(bf16[2,16,512]{2,1,0:T(8,128)(2,1)} %vec_h.1, bf16[48,2,128,128]{3,2,1,0:T(8,128)(2,1)} %blocks.1, s32[1,48]{1,0:T(1,128)} %bitcast.3, s32[1,48]{1,0:T(1,128)} %bitcast.4, bf16[2,32,512]{2,1,0:T(8,128)(2,1)} %rowb_h.1, bf16[2,32,512]{2,1,0:T(8,128)(2,1)} %colb_h.1, ...), custom_call_target="tpu_custom_call" | custom-call | tf_op jit(solution)/shard_map/operator/pallas_call | solution.py:386
  30.1 1.4 %copy.12 = bf16[2,16,512]{2,1,0:T(8,128)(2,1)} copy(bf16[2,16,512]{2,1,0:T(8,128)(2,1)} %get-tuple-element.4) | data formatting | bytes 65536
  31.5 1.4 %copy.13 = bf16[2,16,512]{2,1,0:T(8,128)(2,1)} copy(bf16[2,16,512]{2,1,0:T(8,128)(2,1)} %get-tuple-element.5) | data formatting | bytes 65536

commit v3 on v2

--- a/solution.py
+++ b/solution.py
@@ -20,7 +20,7 @@
     out0, out1,
     vec, rows, cols, rowb, colb, coup, farc, in_sem,
     blk, blk_sem, idx_v, idx_s, idx_sem, wcol, wcoup, xw0, xw1, xrs, xss, fss,
-    csend, crecv, crs, css, coef0, coef1, grs, gss,
+    crecv, crs, css, coef0, coef1,
     dsend, drecv, drs, dss, sums, nown, nsend, nrecv, nrs, nss,
 ):
     t = lax.axis_index("clus")
@@ -34,6 +34,8 @@
     nb = blk.shape[0]
     part = nb // CHUNKS
     far_dev = coup.shape[0]
+    rank_size = coup.shape[2]
+    half = 2 * rank_size
     partner = 2 * g + 1 - c
 
     vec_in, rows_in, cols_in, farc_in, colb_in, coup_in, rowb_in = [
@@ -65,6 +67,19 @@
             device_id={"clus": tt, "sub": ss}, device_id_type=pl.DeviceIdType.MESH,
         )
 
+    mates = clus_count * sub_count - 1
+
+    def mate(i):
+        d, j = i // sub_count, i % sub_count
+        return lax.rem(t + d, clus_count), lax.rem(s + j, sub_count)
+
+    def each(act):
+        if mates < 32:
+            for i in range(1, mates + 1):
+                act(i)
+        else:
+            lax.fori_loop(1, mates + 1, lambda i, state: (act(i), state)[1], 0)
+
     barrier = pltpu.get_barrier_semaphore()
 
     def greet(tt, ss):
@@ -72,25 +87,7 @@
             barrier, inc=1, device_id={"clus": tt, "sub": ss}, device_id_type=pl.DeviceIdType.MESH
         )
 
-    for j in range(1, sub_count):
-        greet(t, lax.rem(s + j, sub_count))
-    expected = sub_count - 1
-    for dt in (-1, 1):
-        @pl.when(has(dt))
-        def _(dt=dt):
-            for j in range(groups):
-                greet(t + dt, 2 * lax.rem(g + j, groups) + c)
-
-        expected = expected + jnp.where(has(dt), groups, 0)
-    for d in range(2, clus_count):
-        for sign in (-1, 1):
-            ok = (t - d >= 0) if sign < 0 else (t + d < clus_count)
-
-            @pl.when(ok)
-            def _(d=d, sign=sign):
-                greet(t + sign * d, s)
-
-            expected = expected + jnp.where(ok, 1, 0)
+    each(lambda i: greet(*mate(i)))
 
     def slot(w, ss):
         return pl.ds((w * sub_count + ss) * leaf_dev, leaf_dev)
@@ -131,11 +128,12 @@
         [
             jnp.concatenate([colb[0], -colb[1]], axis=1),
             jnp.concatenate([colb[1], colb[0]], axis=1),
+            jnp.zeros((wcol.shape[0] - 2 * rank_size, wcol.shape[1]), BF16),
         ],
         axis=0,
     )
 
-    pl.semaphore_wait(barrier, expected)
+    pl.semaphore_wait(barrier, mates)
 
     for prod in range(2):
         x = vec if prod == 0 else out0
@@ -173,52 +171,41 @@
 
         lhs = jnp.concatenate([x[0], x[1]], axis=1)
         partial = lax.dot_general(lhs, wcol[...], NT, preferred_element_type=F32)
-        csend[prod] = partial
-
-        def coef_send(j, prod=prod):
-            return remote(
-                csend.at[prod], crecv.at[prod, s], css.at[prod, j], crs.at[prod, s],
-                t, lax.rem(s + j, sub_count),
-            )
-
-        def coef_recv(j, prod=prod):
-            ss = lax.rem(s + j, sub_count)
-            return remote(
-                csend.at[prod], crecv.at[prod, ss], css.at[prod, j], crs.at[prod, ss], t, ss
-            )
-
-        for j in range(1, sub_count):
-            coef_send(j).start()
+        me = t * sub_count + s
+        crecv[prod, me] = jnp.concatenate(
+            [partial[: rhs // 2, :half], partial[rhs // 2 :, :half]], axis=1
+        )
+
+        def coef_send(i, prod=prod, me=me):
+            tt, ss = mate(i)
+            return remote(
+                crecv.at[prod, me], crecv.at[prod, me], css.at[prod, i], crs.at[prod, me], tt, ss
+            )
+
+        def coef_recv(i, prod=prod):
+            tt, ss = mate(i)
+            here = tt * sub_count + ss
+            return remote(
+                crecv.at[prod, here], crecv.at[prod, here], css.at[prod, i], crs.at[prod, here],
+                tt, ss,
+            )
+
+        each(lambda i: coef_send(i).start())
         if prod == 0:
             coup_in.wait()
             rowb_in.wait()
             idx_copy.wait()
+            wcoup[...] = jnp.zeros(wcoup.shape, BF16)
+            coef0[...] = jnp.zeros(coef0.shape, BF16)
+            coef1[...] = jnp.zeros(coef1.shape, BF16)
             for f in range(far_dev):
-                wcoup[f] = jnp.concatenate(
+                wcoup[f, : 2 * rank_size, : 2 * rank_size] = jnp.concatenate(
                     [
                         jnp.concatenate([coup[f, 0], -coup[f, 1]], axis=1),
                         jnp.concatenate([coup[f, 1], coup[f, 0]], axis=1),
                     ],
                     axis=0,
                 )
-        for j in range(1, sub_count):
-            coef_recv(j).wait_recv()
-            partial = partial + crecv[prod, lax.rem(s + j, sub_count)]
-        coef[t] = partial.astype(BF16)
-
-        def gather_send(d, prod=prod, coef=coef):
-            return remote(
-                coef.at[t], coef.at[t], gss.at[prod, d], grs.at[prod, t],
-                lax.rem(t + d, clus_count), s,
-            )
-
-        def gather_recv(d, prod=prod, coef=coef):
-            tt = lax.rem(t + d, clus_count)
-            return remote(coef.at[tt], coef.at[tt], gss.at[prod, d], grs.at[prod, tt], tt, s)
-
-        for d in range(1, clus_count):
-            gather_send(d).start()
-
         for j in range(groups):
             for dt in (-1, 1):
                 @pl.when(has(dt))
@@ -231,8 +218,14 @@
                 hop.wait_recv()
                 hop.start()
 
-        for d in range(1, clus_count):
-            gather_recv(d).wait_recv()
+        each(lambda i: coef_recv(i).wait_recv())
+        for tt in range(clus_count):
+            packed = crecv[prod, tt * sub_count]
+            for ss in range(1, sub_count):
+                packed = packed + crecv[prod, tt * sub_count + ss]
+            coef[tt, :, :half] = jnp.concatenate(
+                [packed[:, :half], packed[:, half:]], axis=0
+            ).astype(BF16)
         coupled = jnp.zeros(partial.shape, F32)
         for f in range(far_dev):
             coupled = coupled + lax.dot_general(
@@ -312,8 +305,7 @@
             coupled_recv(j).wait_recv()
             coupled = coupled + drecv[prod, lax.rem(s + j, sub_count)]
         coupled = coupled.astype(BF16)
-        rank_size = coupled.shape[1] // 2
-        c0, c1 = coupled[:, :rank_size], coupled[:, rank_size:]
+        c0, c1 = coupled[:, :rank_size], coupled[:, rank_size : 2 * rank_size]
         left = jnp.concatenate(
             [jnp.concatenate([c0, -c1], axis=1), jnp.concatenate([c1, c0], axis=1)], axis=0
         )
@@ -340,7 +332,6 @@
 
     for prod in range(2):
         xw = (xw0, xw1)[prod]
-        coef = (coef0, coef1)[prod]
 
         def sent(src, sem):
             remote(src, src, sem, sem, t, partner).wait_send()
@@ -357,10 +348,8 @@
                 ss = 2 * lax.rem(g + j, groups) + c
                 sent(xw.at[slot(1, ss)], fss.at[prod, 1, j])
         for j in range(1, sub_count):
-            sent(csend.at[prod], css.at[prod, j])
             sent(dsend.at[prod], dss.at[prod, j])
-        for d in range(1, clus_count):
-            sent(coef.at[t], gss.at[prod, d])
+        each(lambda i, prod=prod: sent(crecv.at[prod, t * sub_count + s], css.at[prod, i]))
         for jg in range(groups):
             for e in range(2):
                 if (jg, e) != (0, 0):
@@ -381,13 +370,14 @@
     rank = row_basis.shape[1]
     far_dev = couplings.shape[0]
     dma = pltpu.SemaphoreType.DMA
-    small = (rhs, 2 * rank)
+    width = -(-2 * rank // 128) * 128
+    small = (rhs, width)
     vmem = pl.BlockSpec(memory_space=pltpu.VMEM)
     return pl.pallas_call(
         functools.partial(kernel, clus_count, sub_count, leaf_size),
         out_shape=(
-            jax.ShapeDtypeStruct(vector.shape, BF16),
-            jax.ShapeDtypeStruct(vector.shape, BF16),
+            pltpu.VMEM(vector.shape, BF16),
+            pltpu.VMEM(vector.shape, BF16),
         ),
         in_specs=[pl.BlockSpec(memory_space=pl.ANY)] * 8,
         out_specs=(vmem, vmem),
@@ -398,15 +388,14 @@
             pltpu.VMEM((1, far_dev), jnp.int32), dma((7,)),
             pltpu.VMEM(near_blocks.shape, BF16), dma((CHUNKS,)),
             pltpu.VMEM((8, 128), jnp.int32), pltpu.SMEM((8, 128), jnp.int32), dma(()),
-            pltpu.VMEM((2 * rank, 2 * rows_dev), BF16),
-            pltpu.VMEM((far_dev, 2 * rank, 2 * rank), BF16),
+            pltpu.VMEM((width, 2 * rows_dev), BF16),
+            pltpu.VMEM((far_dev, width, width), BF16),
             pltpu.VMEM((window, 2, rhs, leaf_size), BF16),
             pltpu.VMEM((window, 2, rhs, leaf_size), BF16),
             dma((2, 3, sub_count)), dma((2, 3, groups)), dma((2, 3, groups)),
-            pltpu.VMEM((2,) + small, F32), pltpu.VMEM((2, sub_count) + small, F32),
-            dma((2, sub_count)), dma((2, sub_count)),
+            pltpu.VMEM((2, clus_count * sub_count, rhs // 2, 4 * rank), F32),
+            dma((2, clus_count * sub_count)), dma((2, clus_count * sub_count)),
             pltpu.VMEM((clus_count,) + small, BF16), pltpu.VMEM((clus_count,) + small, BF16),
-            dma((2, clus_count)), dma((2, clus_count)),
             pltpu.VMEM((2,) + small, F32), pltpu.VMEM((2, sub_count) + small, F32),
             dma((2, sub_count)), dma((2, sub_count)),
             pltpu.VMEM((nb + 1, 2 * rhs, leaf_size), F32),

time: 33.1 us -> 30.2 us (0.912)
  local copies, waits for them, and re-layouts: 2.75 us -> 1.23 us
  Pallas kernels: 29.4 us -> 28.2 us
    unnamed x2, local copies, waits for them, and re-layouts: 2.75 us -> 1.23 us
    pallas_call x1, Pallas kernels: 29.4 us -> 28.2 us  [per_device(): pl.pallas_call(functools.partial(kernel, clus_count, sub_count, leaf_size...]
where the time goes in v3:
time: 30.2 us; the launch traced here: 30.1 us
  Pallas kernels  28.2 us (93%)
  local copies, waits for them, and re-layouts  1.23 us (4%)
  between operations  0.64 us (2%)
    pallas_call x1, Pallas kernels, per_device(): pl.pallas_call(functools.partial(kernel, clus_count, sub_count, leaf_size...  28.2 us
    unnamed x2, local copies, waits for them, and re-layouts  1.23 us

profile of v3, /device:TPU:0, one launch (start us, length us, event | category | flops | bytes accessed | tf_op | source)
XLA Modules:
  0.0 30.1 jit_solution(9972007880921831338)
XLA Ops:
  0.6 28.2 %operator.1 = (bf16[2,16,512]{2,1,0:T(8,128)(2,1)S(1)}, bf16[2,16,512]{2,1,0:T(8,128)(2,1)S(1)}) custom-call(bf16[2,16,512]{2,1,0:T(8,128)(2,1)} %vec_h.1, bf16[48,2,128,128]{3,2,1,0:T(8,128)(2,1)} %blocks.1, s32[1,48]{1,0:T(1,128)} %bitcast.3, s32[1,48]{1,0:T(1,128)} %bitcast.4, bf16[2,32,512]{2,1,0:T(8,128)(2,1)} %rowb_h.1, bf16[2,32,512]{2,1,0:T(8,128)(2,1)} %colb_h.1, ...), custom_call_target="tpu_custom_call" | custom-call | tf_op jit(solution)/shard_map/operator/pallas_call | solution.py:376
  28.8 0.6 %copy.12 = bf16[2,16,512]{2,1,0:T(8,128)(2,1)} copy(bf16[2,16,512]{2,1,0:T(8,128)(2,1)S(1)} %get-tuple-element.2) | data formatting | bytes 65536
  29.5 0.6 %copy.13 = bf16[2,16,512]{2,1,0:T(8,128)(2,1)} copy(bf16[2,16,512]{2,1,0:T(8,128)(2,1)S(1)} %get-tuple-element.3) | data formatting | bytes 65536
